TPU v7x, 32 devices: a whole 2x2x4 slice. The times are simulated.
32 devices in a mesh: dp: 4 (over y, x), row: 4 (over z), col: 2 (over core).
Axes of the slice: x: 2, y: 2, z: 4, core: 2. Of those that a mesh axis runs over, the one named last changes fastest.
Arguments:
- activations: bfloat16 [7168, 6144], P(('dp', 'row'), 'col'), may hold values from -6 to 6
- cotangent: bfloat16 [7168, 12288], P(('dp', 'col'), 'row'), may hold values from -6 to 6
- preact: bfloat16 [7168, 12288], P(('dp', 'col'), 'row'), may hold values from -6 to 6
- weight: bfloat16 [6144, 12288], P('col', 'row'), may hold values from -0.078125 to 0.078125
- adapter_input_weight: bfloat16 [3, 32, 6144], P(None, None, 'col'), may hold values from -0.078125 to 0.078125
- adapter_output_weight: bfloat16 [3, 32, 12288], P(None, None, 'row'), may hold values from -1 to 1
- owner: int32 [4], replicated, may hold values from 0 to 2, as said below
Outputs:
- grad_input: bfloat16 [7168, 6144], P(('dp', 'row'), 'col')
- grad_weight: bfloat16 [6144, 12288], P('col', 'row')
- lora_in_grad: float32 [3, 32, 6144], P(None, None, 'col')
- lora_out_grad: float32 [3, 32, 12288], P(None, None, 'row')
Inputs may be any that keep to these rules, and one draw needn't show every extreme that they name: `owner`: customer of each index of dp; each of the 3 customers owns at least one index, so some own several.
All inputs are finite; a program needn't handle non-finite values.
Results may differ from a plain program's by a relative error of at most 0.024.
Values may be sent and summed in bfloat16 or wider, within the bound.
No kernel may reach another device: no remote copies, remote signals or barrier semaphores. Data moves between devices by JAX's collectives and lax.ppermute only.
A program may use at most 192 MiB of HBM per device.

v0:
```python
import jax
import jax.numpy as jnp
from jax import lax
from jax.sharding import PartitionSpec as P

CUSTOMER_COUNT = 3


adapter_scale_factor = 2.0


def gelu_slope(value):
    return (
        0.5 * (1.0 + lax.erf(value * 0.7071067811865476))
        + value * jnp.exp(-0.5 * value * value) * 0.3989422804014327
    )


def local(
    activations, cotangent, preact, weight, adapter_input_weight, adapter_output_weight, owner
):
    client_index = owner[lax.axis_index("dp")]
    rank_down_result = lax.dynamic_index_in_dim(
        adapter_input_weight, client_index, 0, keepdims=False
    )
    rank_upward_result = lax.dynamic_index_in_dim(
        adapter_output_weight, client_index, 0, keepdims=False
    )
    wide_down_result = rank_down_result.astype(jnp.float32)
    owner_mask = (jnp.arange(CUSTOMER_COUNT) == client_index).astype(jnp.float32)
    grad_pre = (cotangent.astype(jnp.float32) * gelu_slope(preact.astype(jnp.float32))).astype(
        jnp.bfloat16
    )
    every_gradient = lax.all_gather(grad_pre, "col", axis=0, tiled=True)
    every_activation = lax.all_gather(activations, "row", axis=0, tiled=True)
    rank_everything = jnp.dot(
        every_gradient, rank_upward_result.T, preferred_element_type=jnp.float32
    )
    rank_activation = lax.psum(
        jnp.dot(every_activation, rank_down_result.T, preferred_element_type=jnp.float32).astype(
            jnp.bfloat16
        ),
        "col",
    )
    output_adapter_term = adapter_scale_factor * jnp.dot(
        rank_activation.T, every_gradient, preferred_element_type=jnp.float32
    )
    out_slots = owner_mask[:, None, None] * output_adapter_term[None]
    incomplete_term = jnp.dot(every_gradient, weight.T, preferred_element_type=jnp.float32)
    grad_input = lax.psum_scatter(
        (
            incomplete_term
            + adapter_scale_factor
            * jnp.dot(rank_everything, wide_down_result, precision=lax.Precision.HIGHEST)
        ).astype(jnp.bfloat16),
        "row",
        scatter_dimension=0,
        tiled=True,
    )
    rank_gradient = lax.psum(rank_everything.astype(jnp.bfloat16), "row")
    input_adapter_term = adapter_scale_factor * jnp.dot(
        rank_gradient.T, every_activation, preferred_element_type=jnp.float32
    )
    in_slots = owner_mask[:, None, None] * input_adapter_term[None]
    in_total, out_total = (
        lax.psum(in_slots.astype(jnp.bfloat16), "dp").astype(jnp.float32),
        lax.psum(out_slots.astype(jnp.bfloat16), "dp").astype(jnp.float32),
    )
    weight_term = lax.dot_general(
        every_activation,
        every_gradient,
        (((0,), (0,)), ((), ())),
        preferred_element_type=jnp.float32,
    )
    grad_weight = lax.psum(weight_term.astype(jnp.bfloat16), "dp")
    return (grad_input, grad_weight, in_total, out_total)


def solution(mesh):
    placed = (
        P(("dp", "row"), "col"),
        P(("dp", "col"), "row"),
        P(("dp", "col"), "row"),
        P("col", "row"),
        P(None, None, "col"),
        P(None, None, "row"),
        P(),
    )
    return jax.shard_map(
        local,
        mesh=mesh,
        in_specs=placed,
        out_specs=(
            P(("dp", "row"), "col"),
            P("col", "row"),
            P(None, None, "col"),
            P(None, None, "row"),
        ),
        check_vma=False,
    )
```

profile of v0, /device:TPU:0, one launch (start us, length us, event | category | flops | bytes accessed | tf_op | source)
XLA Modules:
  0.0 860.8 jit_solution(16800872643333726114)
XLA Ops:
  7.2 0.0 copy-start
  7.2 0.0 copy-start.4
  7.2 0.0 all-gather.3.cloned.1.call-start
  7.2 9.2 %fusion.7 = bf16[896,3072]{1,0:T(8,128)(2,1)} fusion(bf16[896,3072]{1,0:T(8,128)(2,1)} %param.9, bf16[896,3072]{1,0:T(8,128)(2,1)} %param.8), kind=kLoop, calls=%fused_computation.13 | loop fusion | flops 33030144 | bytes 16515072 | tf_op jit(solution)/shard_map/convert_element_type | solution.py:31
  16.5 0.0 all-gather.3.cloned.1.call-update
  16.5 0.0 all-gather.5.cloned.1.call-start
  16.6 0.7 all-gather.5.cloned.1.call-update
  17.3 0.0 all-reduce.5.cloned.1.call-start
  17.3 0.0 copy-done.4
  17.3 0.6 dynamic_slice.10
  19.8 0.6 compare_convert_fusion
  20.5 22.3 %all-gather.3.cloned.1.call-done = bf16[1792,3072]{1,0:T(8,128)(2,1)} async-done(((bf16[896,3072]{1,0:T(8,128)(2,1)}), bf16[1792,3072]{1,0:T(8,128)(2,1)}) %all-gather.3.cloned.1.call-update) | async-done | bytes 11010064 | tf_op jit(solution)/shard_map/all_gather | solution.py:34
  42.8 8.1 fusion.20
  50.9 0.0 all-reduce.5.cloned.1.call-update
  50.9 0.0 all-reduce.7.cloned.1.call-start
  51.0 187.1 %all-gather.5.cloned.1.call-done = bf16[1792,3072]{1,0:T(8,128)(2,1)} async-done(((bf16[448,3072]{1,0:T(8,128)(2,1)}), bf16[1792,3072]{1,0:T(8,128)(2,1)}) %all-gather.5.cloned.1.call-update) | async-done | bytes 11010064 | tf_op jit(solution)/shard_map/all_gather | solution.py:35
  238.0 0.0 copy-done
  238.0 8.1 fusion.8
  246.2 0.0 all-reduce.7.cloned.1.call-update
  246.2 0.2 all-reduce.9.cloned.1.call-start
  246.4 42.1 %convert_bitcast_fusion = bf16[3072,3072]{0,1:T(8,128)(2,1)} fusion(bf16[1792,3072]{1,0:T(8,128)(2,1)} %all-gather.3.cloned.1.call-done, bf16[1792,3072]{1,0:T(8,128)(2,1)} %all-gather.5.cloned.1.call-done), kind=kOutput, calls=%fused_computation.5 | convolution fusion | flops 33832304640 | bytes 40894464 | tf_op jit(solution)/shard_map/dot_general | solution.py:69
  288.5 0.0 all-reduce.5.cloned.1.call-done
  288.5 6.3 convolution_multiply_fusion.1
  294.8 0.0 all-reduce.7.cloned.1.call-done
  294.8 6.2 convolution_multiply_fusion
  301.0 1.3 multiply_convert_fusion
  302.3 0.0 all-reduce.9.cloned.1.call-update
  302.3 0.3 reduce-scatter.2.cloned.1.call-start
  302.5 12.4 %fusion.10 = f32[1792,3072]{1,0:T(8,128)} fusion(f32[1792,32]{0,1:T(8,128)S(1)} %get-tuple-element.14, bf16[3,32,3072]{2,1,0:T(8,128)(2,1)S(1)} %copy-done, s32[]{:T(128)S(6)} %select_n.9), kind=kOutput, calls=%fused_computation.21 | convolution fusion | flops 2113929216 | bytes 22446084 | tf_op jit(solution)/shard_map/dot_general | solution.py:54
  315.0 43.6 %add_convert_fusion = bf16[1792,3072]{1,0:T(8,128)(2,1)} fusion(f32[1792,3072]{1,0:T(8,128)} %fusion.10, bf16[1792,3072]{1,0:T(8,128)(2,1)} %all-gather.3.cloned.1.call-done, bf16[3072,3072]{1,0:T(8,128)(2,1)} %param.10), kind=kOutput, calls=%fused_computation | convolution fusion | flops 33839382528 | bytes 62914560 | tf_op jit(solution)/shard_map/dot_general | solution.py:49
  358.6 0.0 reduce-scatter.2.cloned.1.call-update
  358.6 306.0 %all-reduce.9.cloned.1.call-done = (bf16[3072,3072]{0,1:T(8,128)(2,1)}, bf16[3,32,3072]{2,1,0:T(8,128)(2,1)}, bf16[3,32,3072]{2,1,0:T(8,128)(2,1)}) async-done(((bf16[3072,3072]{0,1:T(8,128)(2,1)}, bf16[3,32,3072]{2,1,0:T(8,128)(2,1)}, bf16[3,32,3072]{2,1,0:T(8,128)(2,1)}), (bf16[3072,3072]{0,1:T(8,128)(2,1)}, bf16[3,32,3072]{2,1,0:T(8,128)(2,1)}, ...) | async-done | bytes 20054032 | tf_op jit(solution)/shard_map/psum | solution.py:75
  664.7 0.0 copy-start.3
  664.7 0.0 copy-start.2
  664.7 0.0 copy-start.1
  664.7 23.4 %copy.11 = bf16[3072,3072]{1,0:T(8,128)(2,1)} copy(bf16[3072,3072]{0,1:T(8,128)(2,1)} %get-tuple-element.8) | data formatting | bytes 37748736
  688.1 0.0 copy-done.3
  688.1 1.1 convert_element_type.56
  689.2 0.0 copy-done.2
  689.2 1.1 convert_element_type.60
  690.4 163.6 %reduce-scatter.2.cloned.1.call-done = bf16[448,3072]{1,0:T(8,128)(2,1)} async-done(((bf16[1792,3072]{1,0:T(8,128)(2,1)}), bf16[448,3072]{1,0:T(8,128)(2,1)}) %reduce-scatter.2.cloned.1.call-update) | async-done | bytes 2752528 | tf_op jit(solution)/shard_map/reduce_scatter | solution.py:50
  853.9 0.0 copy-done.1
Async XLA Ops:
  7.2 230.9 %copy-start = (bf16[3,32,3072]{2,1,0:T(8,128)(2,1)S(1)}, bf16[3,32,3072]{2,1,0:T(8,128)(2,1)}, u32[]{:S(2)}) copy-start(bf16[3,32,3072]{2,1,0:T(8,128)(2,1)} %param.11) | copy-start | bytes 1769476
  7.2 10.1 %copy-start.4 = (s32[4]{0:T(128)S(1)}, s32[4]{0:T(128)}, u32[]{:S(2)}) copy-start(s32[4]{0:T(128)} %param.13) | copy-start | bytes 52
  7.2 35.6 %all-gather.3.cloned.1.call-start = ((), (), s32[]{:S(2)}) async-start(), calls=%async_computation.1 | async-start | bytes 16515072 | tf_op jit(solution)/shard_map/all_gather | solution.py:34
  16.5 221.5 %all-gather.5.cloned.1.call-start = ((), (), s32[]{:S(2)}) async-start(), calls=%async_computation.3 | async-start | bytes 13762560 | tf_op jit(solution)/shard_map/all_gather | solution.py:35
  17.3 271.3 %all-reduce.5.cloned.1.call-start = ((), (), s32[]{:S(2)}) async-start(), calls=%async_computation.4 | async-start | bytes 229376 | tf_op jit(solution)/shard_map/psum | solution.py:60
  50.9 243.9 %all-reduce.7.cloned.1.call-start = ((), (), s32[]{:S(2)}) async-start(), calls=%async_computation.5 | async-start | bytes 229376 | tf_op jit(solution)/shard_map/psum | solution.py:39
  246.2 418.5 %all-reduce.9.cloned.1.call-start = ((), (), s32[]{:S(2)}) async-start(), calls=%async_computation.6 | async-start | bytes 40108032 | tf_op jit(solution)/shard_map/psum | solution.py:75
  302.3 551.7 %reduce-scatter.2.cloned.1.call-start = ((), (), s32[]{:S(2)}) async-start(), calls=%async_computation.2 | async-start | bytes 13762560 | tf_op jit(solution)/shard_map/reduce_scatter | solution.py:50
  664.7 23.4 %copy-start.3 = (bf16[3,32,3072]{2,1,0:T(8,128)(2,1)S(1)}, bf16[3,32,3072]{2,1,0:T(8,128)(2,1)}, u32[]{:S(2)}) copy-start(bf16[3,32,3072]{2,1,0:T(8,128)(2,1)} %get-tuple-element.9) | copy-start | bytes 1769476
  664.7 24.6 %copy-start.2 = (bf16[3,32,3072]{2,1,0:T(8,128)(2,1)S(1)}, bf16[3,32,3072]{2,1,0:T(8,128)(2,1)}, u32[]{:S(2)}) copy-start(bf16[3,32,3072]{2,1,0:T(8,128)(2,1)} %get-tuple-element.10) | copy-start | bytes 1769476
  664.7 189.3 %copy-start.1 = (bf16[3,32,3072]{2,1,0:T(8,128)(2,1)S(1)}, bf16[3,32,3072]{2,1,0:T(8,128)(2,1)}, u32[]{:S(2)}) copy-start(bf16[3,32,3072]{2,1,0:T(8,128)(2,1)} %param.11) | copy-start | bytes 1769476
Sparse Core Ops, SparseCore 0:
  16.6 26.1 all-gather.2
  44.3 193.6 all-gather.4
  240.9 32.2 all-reduce.4
  276.1 17.8 all-reduce.6
  302.4 362.2 all-reduce.8
  667.5 186.4 reduce-scatter.1
where the time goes:
time: 862 us; the launch traced here: 861 us
  waiting for transfers between devices  680 us (79%)
  matrix products  127 us (15%)
  local copies, waits for them, and re-layouts  24 us (3%)
  between operations  16.1 us (2%)
  other arithmetic  13.4 us (2%)
    psum x1, waiting for transfers between devices, local(): grad_weight = lax.psum(weight_term.astype(jnp.bfloat16), 'dp')  306 us
    all_gather x1, waiting for transfers between devices, local(): every_activation = lax.all_gather(activations, 'row', axis=0, tiled=True)  187 us
    reduce_scatter x1, waiting for transfers between devices, local(): lax.psum_scatter((incomplete_term + adapter_scale_factor * jnp.dot(rank_e...  164 us
    dot_general x1, matrix products, local(): jnp.dot(every_gradient, weight.T, preferred_element_type=jnp.float32)  43.6 us
    dot_general x1, matrix products, local(): lax.dot_general(every_activation, every_gradient, (((0,), (0,)), ((), ())...  42.1 us
    unnamed x11, local copies, waits for them, and re-layouts  23.5 us
    all_gather x1, waiting for transfers between devices, local(): every_gradient = lax.all_gather(grad_pre, 'col', axis=0, tiled=True)  22.3 us
  transfers between devices with their start and end apart: 6, of which 4 were waited for; matrix products, arithmetic and copies ran while one was open for 17% of the time, Pallas kernels for 0%

commit v1 on v0

v1 whole, which is shorter than its diff:
```python
import jax
import jax.numpy as jnp
from jax import lax
from jax.experimental import pallas as pl
from jax.experimental.pallas import tpu as pltpu
from jax.sharding import PartitionSpec as P

CUSTOMER_COUNT = 3
VMEM_LIMIT = 60 * 1024 * 1024
CHUNKS = (2, 2, 3, 3, 2)
LOW_CHUNK = 2

adapter_scale_factor = 2.0


def gelu_slope(value):
    return (
        0.5 * (1.0 + lax.erf(value * 0.7071067811865476))
        + value * jnp.exp(-0.5 * value * value) * 0.3989422804014327
    )


def cost(flops, moved):
    return pl.CostEstimate(flops=3 * flops, bytes_accessed=3 * moved, transcendentals=0)


def anywhere(count):
    return [pl.BlockSpec(memory_space=pl.ANY)] * count


def cut_columns(source, start, width, more, earlier):
    rows = source.shape[0]
    total = width + sum(piece.shape[1] for piece in more)

    def body(source_ref, *refs):
        out, one = refs[-2:]
        one[...] = jnp.ones_like(one)
        out[:, :width] = source_ref[:, start : start + width]
        if more:
            out[:, width:] = refs[0][...]

    return pl.pallas_call(
        body,
        grid=(1,),
        in_specs=[pl.BlockSpec(source.shape, lambda step: (0, 0))]
        + [pl.BlockSpec(piece.shape, lambda step: (0, 0)) for piece in more]
        + anywhere(len(earlier)),
        out_specs=[
            pl.BlockSpec((rows, total), lambda step: (0, 0)),
            pl.BlockSpec((8, 128), lambda step: (0, 0)),
        ],
        out_shape=[
            jax.ShapeDtypeStruct((rows, total), source.dtype),
            jax.ShapeDtypeStruct((8, 128), jnp.float32),
        ],
        compiler_params=pltpu.CompilerParams(vmem_limit_bytes=VMEM_LIMIT),
        cost_estimate=cost(0, 4 * rows * total),
        name="cut_columns",
    )(source, *more, *earlier)


def weight_chunk(choice, act, own, other, features, rank, extra, earlier):
    total = act.shape[1]
    half, hidden = own.shape
    cut = hidden // 8
    block = 2 * cut
    below = sum(CUSTOMER_COUNT * blocks.shape[1] for blocks in extra)
    shapes = [(features + below, block)] * 2 + [(features + below, cut)] * 4
    more = [(8, rank, cut)] if rank else []

    def body(choice_ref, *refs):
        (act_ref, own_ref, other_ref), extra_refs = refs[:3], refs[3 : 3 + len(extra)]
        refs = refs[3 + len(extra) + len(earlier) :]
        outs, refs = refs[: len(shapes)], refs[len(shapes) :]
        low_outs, refs = refs[: len(more)], refs[len(more) :]
        bufs, (act, turned, grad, act_sems, grad_sems, out_sems) = refs[:6], refs[6:]
        step = pl.program_id(0)

        def act_copy(part):
            place = choice_ref[0] if part == 0 else 1 - choice_ref[0]
            return pltpu.make_async_copy(
                act_ref.at[pl.ds(pl.multiple_of(place * half, half), half)],
                act.at[pl.ds(part * half, half)],
                act_sems.at[part],
            )

        def fill(buf, pair, numbers):
            if not extra:
                return
            buf[features:] = jnp.zeros((below, buf.shape[1]), jnp.bfloat16)
            first = features
            for ref in extra_refs:
                size = ref.shape[1]
                place = pl.ds(pl.multiple_of(first + choice_ref[1] * size, size), size)
                for number in numbers:
                    column = 0 if len(numbers) == 1 else number * cut
                    value = adapter_scale_factor * ref[choice_ref[2 + 2 * pair + number]]
                    buf[place, column : column + cut] = value.astype(jnp.bfloat16)
                first += CUSTOMER_COUNT * size

        def grad_copy(number, part):
            columns = pl.ds(pl.multiple_of(choice_ref[2 + number] * cut, cut), cut)
            return pltpu.make_async_copy(
                (own_ref, other_ref)[part].at[:, columns],
                grad.at[number // 2, pl.ds(part * half, half), pl.ds(number % 2 * cut, cut)],
                grad_sems.at[number, part],
            )

        def out_copy(index):
            return pltpu.make_async_copy(bufs[index], outs[index], out_sems.at[index])

        @pl.when(step == 0)
        def _():
            for part in range(2):
                act_copy(part).start()
            for number in range(8):
                for part in range(2):
                    grad_copy(number, part).start()
            for part in range(2):
                act_copy(part).wait()
            turned[...] = act[...].T

        for pair in range(4):

            @pl.when(step == pair)
            def _():
                for number in (2 * pair, 2 * pair + 1):
                    for part in range(2):
                        grad_copy(number, part).wait()
                part = jnp.dot(turned[...], grad[pair], preferred_element_type=jnp.float32)
                for low_out in low_outs:
                    for number in range(2):
                        low_out[choice_ref[2 + 2 * pair + number]] = part[
                            features : features + rank, number * cut : (number + 1) * cut
                        ]
                part = part[:features].astype(jnp.bfloat16)
                if pair < 2:
                    bufs[pair][:features] = part
                    fill(bufs[pair], pair, (0, 1))
                    out_copy(pair).start()
                else:
                    for number in range(2):
                        index = 2 * pair - 2 + number
                        bufs[index][:features] = part[:, number * cut : (number + 1) * cut]
                        fill(bufs[index], pair, (number,))
                        out_copy(index).start()

        @pl.when(step == 3)
        def _():
            for index in range(6):
                out_copy(index).wait()

    return pl.pallas_call(
        body,
        grid_spec=pltpu.PrefetchScalarGridSpec(
            num_scalar_prefetch=1,
            grid=(4,),
            in_specs=anywhere(3)
            + [pl.BlockSpec(blocks.shape, lambda step, choice_ref: (0, 0, 0)) for blocks in extra]
            + anywhere(len(earlier)),
            out_specs=anywhere(len(shapes))
            + [pl.BlockSpec(shape, lambda step, choice_ref: (0, 0, 0)) for shape in more],
            scratch_shapes=[pltpu.VMEM(shape, jnp.bfloat16) for shape in shapes]
            + [
                pltpu.VMEM((2 * half, total), jnp.bfloat16),
                pltpu.VMEM((total, 2 * half), jnp.bfloat16),
                pltpu.VMEM((4, 2 * half, block), jnp.bfloat16),
                pltpu.SemaphoreType.DMA((2,)),
                pltpu.SemaphoreType.DMA((8, 2)),
                pltpu.SemaphoreType.DMA((6,)),
            ],
        ),
        out_shape=[jax.ShapeDtypeStruct(shape, jnp.bfloat16) for shape in shapes]
        + [jax.ShapeDtypeStruct(shape, jnp.float32) for shape in more],
        compiler_params=pltpu.CompilerParams(vmem_limit_bytes=VMEM_LIMIT),
        cost_estimate=cost(
            4 * half * total * hidden, 2 * (2 * half * (total + hidden) + total * hidden)
        ),
        name="weight_chunk",
    )(choice.astype(jnp.int32), act, own, other, *extra, *earlier)


def sums(terms, width, joined, earlier):
    rows = terms[0][0][0].shape[0]
    tile = next(size for size in (256, 320, 352, 224, rows) if rows % size == 0)
    arrays = [array for term in terms for array, _ in term]
    firsts = [first for term in terms for _, first in term]

    def spec(first):
        return pl.BlockSpec((tile, width), lambda step: (step, first // width))

    def body(*refs):
        refs, outs = refs[: len(arrays)], refs[len(arrays) + len(earlier) :]
        at = 0
        for index, term in enumerate(terms):
            total = refs[at][...].astype(jnp.float32)
            for ref in refs[at + 1 : at + len(term)]:
                total = total + ref[...].astype(jnp.float32)
            total = total.astype(jnp.bfloat16)
            if joined:
                outs[0][:, index * width : (index + 1) * width] = total
            else:
                outs[index][...] = total
            at += len(term)

    if joined:
        out_specs = [pl.BlockSpec((tile, width * len(terms)), lambda step: (step, 0))]
        out_shape = [jax.ShapeDtypeStruct((rows, width * len(terms)), jnp.bfloat16)]
    else:
        out_specs = [spec(0)] * len(terms)
        out_shape = [jax.ShapeDtypeStruct((rows, width), jnp.bfloat16)] * len(terms)
    return pl.pallas_call(
        body,
        grid=(rows // tile,),
        in_specs=[spec(first) for first in firsts] + anywhere(len(earlier)),
        out_specs=out_specs,
        out_shape=out_shape,
        compiler_params=pltpu.CompilerParams(vmem_limit_bytes=VMEM_LIMIT),
        cost_estimate=cost(0, 2 * rows * width * (len(arrays) + len(terms))),
        name="sums",
    )(*arrays, *earlier)


def assemble(whole, shape, span, pieces, group, earlier):
    start, stop = span
    width = pieces[0].shape[1]
    cut = width // 2
    tile = 256

    def body(group_ref, own_ref, near_ref, far_ref, low_ref, high_ref, *refs):
        out = refs[-1]
        for device in range(4):

            @pl.when(group_ref[0] == device)
            def _():
                for ref, other in ((own_ref, 0), (near_ref, 1), (far_ref, 2)):
                    begin = (device ^ other) * width
                    out[:, begin : begin + width] = ref[...]
                begin = (device ^ 3) * width
                out[:, begin : begin + cut] = low_ref[...]
                out[:, begin + cut : begin + width] = high_ref[...]

    extra = ([] if whole is None else [whole]) + list(earlier)
    return pl.pallas_call(
        body,
        grid_spec=pltpu.PrefetchScalarGridSpec(
            num_scalar_prefetch=1,
            grid=((stop - start) // tile,),
            in_specs=[
                pl.BlockSpec((tile, piece.shape[1]), lambda step, group_ref: (step, 0))
                for piece in pieces
            ]
            + anywhere(len(extra)),
            out_specs=pl.BlockSpec(
                (tile, shape[1]), lambda step, group_ref: (start // tile + step, 0)
            ),
        ),
        out_shape=jax.ShapeDtypeStruct(shape, pieces[0].dtype),
        input_output_aliases={} if whole is None else {1 + len(pieces): 0},
        compiler_params=pltpu.CompilerParams(vmem_limit_bytes=VMEM_LIMIT),
        cost_estimate=cost(0, 16 * (stop - start) * width),
        name="assemble",
    )(jnp.reshape(group, (1,)).astype(jnp.int32), *pieces, *extra)


def adapter_totals(pieces, first, size, group, earlier):
    width = pieces[0].shape[1]
    cut = width // 2

    def body(group_ref, own_ref, near_ref, far_ref, low_ref, high_ref, *refs):
        outs = refs[len(earlier) :]
        for device in range(4):

            @pl.when(group_ref[0] == device)
            def _():
                opposite = (device ^ 3) * width
                for ref, begin in (
                    (own_ref, device * width), (near_ref, (device ^ 1) * width),
                    (far_ref, (device ^ 2) * width), (low_ref, opposite),
                    (high_ref, opposite + cut),
                ):
                    for index, out in enumerate(outs):
                        at = first + index * size
                        value = ref[at : at + size].astype(jnp.float32)
                        out[:, begin : begin + ref.shape[1]] = value

    return pl.pallas_call(
        body,
        grid_spec=pltpu.PrefetchScalarGridSpec(
            num_scalar_prefetch=1,
            grid=(1,),
            in_specs=[
                pl.BlockSpec(piece.shape, lambda step, group_ref: (0, 0)) for piece in pieces
            ]
            + anywhere(len(earlier)),
            out_specs=[pl.BlockSpec((size, 4 * width), lambda step, group_ref: (0, 0))] * 2,
        ),
        out_shape=[jax.ShapeDtypeStruct((size, 4 * width), jnp.float32)] * 2,
        compiler_params=pltpu.CompilerParams(vmem_limit_bytes=VMEM_LIMIT),
        cost_estimate=cost(0, 48 * size * width),
        name="adapter_totals",
    )(jnp.reshape(group, (1,)).astype(jnp.int32), *pieces, *earlier)


def input_part(slots, rows, own, other, weight, down, up, given, begin, end, earlier):
    half, hidden = own.shape
    features = weight.shape[0]
    rank = up.shape[0]
    tile = 512
    first = begin // tile
    low_shapes = [] if given else [(2 * half, 3 * rank)] + [(rows, rank)] * 4

    def body(slots_ref, own_ref, other_ref, weight_ref, down_ref, up_ref, *refs):
        low, refs = refs[0], refs[len(given) + len(earlier) :]
        out, refs, (grad, rounded, sems) = refs[0], refs[1:-3], refs[-3:]
        if not given:
            low, low_outs = refs[0], refs[1:]

        @pl.when(pl.program_id(0) == 0)
        def _():
            copies = [
                pltpu.make_async_copy(
                    ref, grad.at[pl.ds(index * half, half)], sems.at[index]
                )
                for index, ref in enumerate((own_ref, other_ref))
            ]
            for copy in copies:
                copy.start()
            for copy in copies:
                copy.wait()
            if given:
                return
            part = lax.dot_general(
                grad[...], up_ref[...], (((1,), (1,)), ((), ())),
                preferred_element_type=jnp.float32,
            )
            rounded[...] = part.astype(jnp.bfloat16)
            for index, low_out in enumerate(low_outs):
                start = pl.multiple_of(slots_ref[1 + index] * rows, rows)
                low_out[...] = rounded[pl.ds(start, rows), :]
            part = adapter_scale_factor * part
            high = part.astype(jnp.bfloat16)
            rest = part - high.astype(jnp.float32)
            middle = rest.astype(jnp.bfloat16)
            rest = rest - middle.astype(jnp.float32)
            low[:, :rank] = high
            low[:, rank : 2 * rank] = middle
            low[:, 2 * rank :] = rest.astype(jnp.bfloat16)

        total = lax.dot_general(
            grad[...], weight_ref[...], (((1,), (1,)), ((), ())),
            preferred_element_type=jnp.float32,
        )
        downs = jnp.concatenate([down_ref[...]] * 3, axis=0)
        total = total + jnp.dot(low[...], downs, preferred_element_type=jnp.float32)
        total = total.astype(jnp.bfloat16)
        core = slots_ref[0]
        out[pl.ds(pl.multiple_of(core * half, half), half), :] = total[:half]
        out[pl.ds(pl.multiple_of((1 - core) * half, half), half), :] = total[half:]

    return pl.pallas_call(
        body,
        grid_spec=pltpu.PrefetchScalarGridSpec(
            num_scalar_prefetch=1,
            grid=((end - begin) // tile,),
            in_specs=anywhere(2)
            + [
                pl.BlockSpec((tile, hidden), lambda step, slots_ref: (first + step, 0)),
                pl.BlockSpec((rank, tile), lambda step, slots_ref: (0, first + step)),
                pl.BlockSpec((rank, hidden), lambda step, slots_ref: (0, 0)),
            ]
            + [pl.BlockSpec(value.shape, lambda step, slots_ref: (0, 0)) for value in given[:1]]
            + anywhere(len(given[1:]) + len(earlier)),
            out_specs=[pl.BlockSpec((2 * half, tile), lambda step, slots_ref: (0, first + step))]
            + [pl.BlockSpec(shape, lambda step, slots_ref: (0, 0)) for shape in low_shapes],
            scratch_shapes=[
                pltpu.VMEM((2 * half, hidden), jnp.bfloat16),
                pltpu.VMEM((2 * half, rank), jnp.bfloat16),
                pltpu.SemaphoreType.DMA((2,)),
            ],
        ),
        out_shape=[
            jax.ShapeDtypeStruct(shape, jnp.bfloat16)
            for shape in [(2 * half, features)] + low_shapes
        ],
        input_output_aliases={7: 0} if given else {},
        compiler_params=pltpu.CompilerParams(vmem_limit_bytes=VMEM_LIMIT),
        cost_estimate=cost(
            4 * half * (end - begin) * hidden,
            2 * ((end - begin) * hidden + 2 * half * (hidden + end - begin)),
        ),
        name="input_part",
    )(slots.astype(jnp.int32), own, other, weight, down, up, *given, *earlier)


def low_term(low, places, gathered, source, earlier):
    rows, rank = low.shape
    width = source.shape[1]
    last = gathered.shape[1] // 128 - 1

    def body(places_ref, low_ref, *refs):
        total = low_ref[...].astype(jnp.float32)
        for index in range(3):
            columns = slice((index + 1) * rank, (index + 2) * rank)
            total = total + refs[index][:, columns].astype(jnp.float32)
        total = lax.dot_general(
            total.astype(jnp.bfloat16), refs[3][...], (((0,), (0,)), ((), ())),
            preferred_element_type=jnp.float32,
        )
        refs[-1][...] = total.astype(jnp.bfloat16)

    def block(index):
        return pl.BlockSpec((rows, 128), lambda step, places_ref: (places_ref[index], last))

    return pl.pallas_call(
        body,
        grid_spec=pltpu.PrefetchScalarGridSpec(
            num_scalar_prefetch=1,
            grid=(1,),
            in_specs=[pl.BlockSpec(low.shape, lambda step, places_ref: (0, 0))]
            + [block(index) for index in range(3)]
            + [pl.BlockSpec(source.shape, lambda step, places_ref: (0, 0))]
            + anywhere(len(earlier)),
            out_specs=pl.BlockSpec((rank, width), lambda step, places_ref: (0, 0)),
        ),
        out_shape=jax.ShapeDtypeStruct((rank, width), jnp.bfloat16),
        compiler_params=pltpu.CompilerParams(vmem_limit_bytes=VMEM_LIMIT),
        cost_estimate=cost(2 * rank * source.size, 2 * source.size),
        name="low_term",
    )(places.astype(jnp.int32), low, gathered, gathered, gathered, source, *earlier)


def blocks_of(first, second, earlier):
    rank, width = first.shape
    cut = width // 8

    def body(first_ref, second_ref, *refs):
        for index in range(8):
            columns = slice(index * cut, (index + 1) * cut)
            refs[-1][index] = first_ref[:, columns].astype(jnp.float32) + second_ref[
                :, columns
            ].astype(jnp.float32)

    return pl.pallas_call(
        body,
        grid=(1,),
        in_specs=[pl.BlockSpec((rank, width), lambda step: (0, 0))] * 2 + anywhere(len(earlier)),
        out_specs=pl.BlockSpec((8, rank, cut), lambda step: (0, 0, 0)),
        out_shape=jax.ShapeDtypeStruct((8, rank, cut), jnp.float32),
        compiler_params=pltpu.CompilerParams(vmem_limit_bytes=VMEM_LIMIT),
        cost_estimate=cost(0, 8 * rank * width),
        name="blocks_of",
    )(first, second, *earlier)


def fast(
    activations, cotangent, preact, weight, adapter_input_weight, adapter_output_weight, owner
):
    group = lax.axis_index("dp")
    row = lax.axis_index("row")
    col = lax.axis_index("col")
    near, far = group % 2, group // 2
    client_index = owner[group]
    down = lax.dynamic_index_in_dim(adapter_input_weight, client_index, 0, keepdims=False)
    up = lax.dynamic_index_in_dim(adapter_output_weight, client_index, 0, keepdims=False)
    rows, features = activations.shape
    half, hidden = cotangent.shape
    rank = up.shape[0]
    wide = jnp.float32
    narrow = jnp.bfloat16

    def along(axis, pairs):
        return lambda value: lax.ppermute(value, axis, pairs)

    over_near = along("dp", [(i, i ^ 1) for i in range(4)])
    over_far = along("dp", [(i, i ^ 2) for i in range(4)])
    swap = along("col", [(0, 1), (1, 0)])

    bounds = [0]
    for part in CHUNKS:
        bounds.append(bounds[-1] + features * part // sum(CHUNKS))
    spans = list(zip(bounds[:-1], bounds[1:]))

    def at(shift):
        return (row + shift + 2 * col) % 4

    cuts, acts = {}, {}

    def cut_chunk(index, more, *earlier):
        begin, end = spans[index]
        cuts[index], one = cut_columns(activations, begin, end - begin, more, earlier)
        acts[index] = lax.all_gather(cuts[index], "row", axis=0, tiled=True)
        return one[0, 0]

    one = cut_chunk(0, [])
    cut_chunk(1, [], cuts[0])

    own = (cotangent.astype(wide) * gelu_slope(preact.astype(wide)) * one).astype(narrow)
    other = swap(own)

    over_last = (((1,), (1,)), ((), ()))
    low_act = lax.dot_general(activations, down, over_last, preferred_element_type=wide)
    low_act = low_act.astype(narrow)
    low_act = (low_act.astype(wide) + swap(low_act).astype(wide)).astype(narrow)

    cut = hidden // 8

    def first_kind(a, b):
        return 2 * (a + 2 * b)

    def second_kind(a, b):
        return 2 * (a + 2 * b) + 1

    blocks = jnp.stack([
        first_kind(1 - near, 1 - far), first_kind(1 - near, far),
        second_kind(1 - near, 1 - far), second_kind(near, 1 - far),
        first_kind(near, 1 - far), first_kind(near, far),
        second_kind(1 - near, far), second_kind(near, far),
    ])

    out_term = []
    first, got, kept, sent, more, done, spread, passed = {}, {}, {}, {}, {}, {}, {}, {}
    grad_weight = [None]

    choice = jnp.concatenate([jnp.stack([col, client_index]), blocks])

    def start(index, extra, *earlier):
        begin, end = spans[index]
        to_near, to_far, *kept[index] = weight_chunk(
            choice, acts[index], own, other, end - begin, rank if index == LOW_CHUNK else 0,
            extra, earlier,
        )
        if index == LOW_CHUNK:
            out_term.append(kept[index].pop())
        first[index] = [to_near, to_far]
        got[index] = [over_near(to_near), over_far(to_far)]

    def second(index, *earlier):
        (got_near, got_far), (send_near, _, send_far, _) = got[index], kept[index]
        sent[index] = sums(
            [[(send_near, 0), (got_near, 0)], [(send_far, 0), (got_far, 0)]], cut, False, earlier
        )
        more[index] = [over_far(sent[index][0]), over_near(sent[index][1])]

    def third(index, *earlier):
        (got_near, got_far), (_, keep_near, _, keep_far) = got[index], kept[index]
        done[index] = sums(
            [
                [(keep_near, 0), (got_near, cut), (more[index][0], 0)],
                [(keep_far, 0), (got_far, cut), (more[index][1], 0)],
            ],
            cut, True, earlier,
        )
        (piece,) = done[index]
        spread[index] = [piece, over_near(piece), over_far(piece)]

    def forward(index, *earlier):
        _, from_near, from_far = spread[index]
        passed[index] = sums([[(from_far, 0)], [(from_near, cut)]], cut, False, earlier)
        spread[index] += [over_near(passed[index][0]), over_far(passed[index][1])]

    def finish(index, *earlier):
        grad_weight[0] = assemble(
            grad_weight[0], (features, hidden), spans[index], spread[index], group, earlier
        )

    slots = jnp.stack([col, at(0), at(1), at(2), at(3)])
    middle = features // 3
    grads, lows, *low_rows = input_part(
        slots, rows, own, other, weight, down, up, [], 0, middle, [cuts[1]]
    )
    start(0, [], grads)
    cut_chunk(LOW_CHUNK, [jnp.concatenate([low_act, *low_rows[1:]], axis=1)], first[0][0])
    cut_chunk(3, [], cuts[2])
    cut_chunk(4, [], cuts[3])
    second(0, cuts[4])
    third(0, *sent[0])
    start(1, [], *done[0])
    (grads,) = input_part(
        slots, rows, own, other, weight, down, up, [lows, grads], middle, features, first[1]
    )
    grad_input = lax.psum_scatter(grads, "row", scatter_dimension=0, tiled=True)
    forward(0, grads)
    second(1, *passed[0])
    third(1, *sent[1], *spread[0][3:])
    start(2, [], *done[1])
    finish(0, first[2][0])
    in_term = low_term(
        low_rows[0], jnp.stack([(row - shift) % 4 for shift in (1, 2, 3)]), acts[LOW_CHUNK],
        activations, [grad_weight[0]],
    )
    received = along("row", [(i, i ^ 1) for i in range(4)])(in_term)
    forward(1, in_term)
    second(2, *passed[1])
    third(2, *sent[2], *spread[1][3:])
    start(3, [], *done[2])
    finish(1, first[3][0])
    (in_term,) = sums([[(in_term, 0), (received, 0)]], features, False, [grad_weight[0]])
    received = along("row", [(i, i ^ 2) for i in range(4)])(in_term)
    forward(2, in_term)
    second(3, *passed[2])
    in_term = blocks_of(in_term, received, sent[3])
    third(3, in_term, *spread[2][3:])
    start(4, [in_term, out_term[0]], *done[3])
    finish(2, first[4][0])
    forward(3, grad_weight[0])
    second(4, *passed[3])
    third(4, *sent[4], *spread[3][3:])
    finish(3, *done[4])
    forward(4, grad_weight[0])
    finish(4, *passed[4])
    size = CUSTOMER_COUNT * rank
    begin, end = spans[4]
    totals = adapter_totals(spread[4], end - begin, size, group, [grad_weight[0]])
    totals = [total.reshape(CUSTOMER_COUNT, rank, -1) for total in totals]
    return grad_input, grad_weight[0], totals[0], totals[1]


def plain(
    activations, cotangent, preact, weight, adapter_input_weight, adapter_output_weight, owner
):
    client_index = owner[lax.axis_index("dp")]
    down = lax.dynamic_index_in_dim(adapter_input_weight, client_index, 0, keepdims=False)
    up = lax.dynamic_index_in_dim(adapter_output_weight, client_index, 0, keepdims=False)
    owner_mask = (jnp.arange(CUSTOMER_COUNT) == client_index).astype(jnp.float32)
    grad_pre = (cotangent.astype(jnp.float32) * gelu_slope(preact.astype(jnp.float32))).astype(
        jnp.bfloat16
    )
    grad = lax.all_gather(grad_pre, "col", axis=0, tiled=True)
    act = lax.all_gather(activations, "row", axis=0, tiled=True)
    low_part = jnp.dot(grad, up.T, preferred_element_type=jnp.float32)
    low_act = lax.psum(
        jnp.dot(act, down.T, preferred_element_type=jnp.float32).astype(jnp.bfloat16), "col"
    )
    out_term = adapter_scale_factor * jnp.dot(
        low_act.T, grad, preferred_element_type=jnp.float32
    )
    input_part = jnp.dot(grad, weight.T, preferred_element_type=jnp.float32)
    input_part = input_part + adapter_scale_factor * jnp.dot(
        low_part, down.astype(jnp.float32), precision=lax.Precision.HIGHEST
    )
    grad_input = lax.psum_scatter(
        input_part.astype(jnp.bfloat16), "row", scatter_dimension=0, tiled=True
    )
    low_grad = lax.psum(low_part.astype(jnp.bfloat16), "row")
    in_term = adapter_scale_factor * jnp.dot(low_grad.T, act, preferred_element_type=jnp.float32)
    in_slots = owner_mask[:, None, None] * in_term[None]
    out_slots = owner_mask[:, None, None] * out_term[None]
    in_total = lax.psum(in_slots.astype(jnp.bfloat16), "dp").astype(jnp.float32)
    out_total = lax.psum(out_slots.astype(jnp.bfloat16), "dp").astype(jnp.float32)
    weight_term = lax.dot_general(
        act, grad, (((0,), (0,)), ((), ())), preferred_element_type=jnp.float32
    )
    grad_weight = lax.psum(weight_term.astype(jnp.bfloat16), "dp")
    return grad_input, grad_weight, in_total, out_total


def solution(mesh):
    sizes = (mesh.shape["dp"], mesh.shape["row"], mesh.shape["col"])
    placed = (
        P(("dp", "row"), "col"),
        P(("dp", "col"), "row"),
        P(("dp", "col"), "row"),
        P("col", "row"),
        P(None, None, "col"),
        P(None, None, "row"),
        P(),
    )
    return jax.shard_map(
        fast if sizes == (4, 4, 2) else plain,
        mesh=mesh,
        in_specs=placed,
        out_specs=(
            P(("dp", "row"), "col"),
            P("col", "row"),
            P(None, None, "col"),
            P(None, None, "row"),
        ),
        check_vma=False,
    )
```

time: 862 us -> 537 us (0.62)
  waiting for transfers between devices: 680 us -> 212 us
  Pallas kernels: 0 us -> 225 us
  matrix products: 127 us -> 0.86 us
  starting transfers between devices: 0.65 us -> 40.7 us
    psum x3 -> x0, waiting for transfers between devices: 306 us -> none  [the longest x1 306 us: local(): grad_weight = lax.psum(weight_term.astype(jnp.bfloat16), 'dp')]
    pallas_call x0 -> x36, Pallas kernels: none -> 225 us  [the longest x5 78.5 us: weight_chunk(): pl.pallas_call(body, grid_spec=pltpu.PrefetchScalarGridSpec(num_scalar_pr...]
    ppermute x0 -> x44, waiting for transfers between devices: none -> 205 us  [along(): return lambda value: lax.ppermute(value, axis, pairs)]
    all_gather x2 -> x5, waiting for transfers between devices: 209 us -> 6.65 us  [cut_chunk(): acts[index] = lax.all_gather(cuts[index], 'row', axis=0, tiled=True)]
    reduce_scatter x1, waiting for transfers between devices: 164 us -> 0.01 us  [fast(): grad_input = lax.psum_scatter(grads, 'row', scatter_dimension=0, tiled=True)]
    dot_general x7 -> x1, matrix products: 127 us -> 0.86 us  [fast(): lax.dot_general(activations, down, over_last, preferred_element_type=wide)]
    ppermute x0 -> x44, starting transfers between devices: none -> 40.3 us  [along(): return lambda value: lax.ppermute(value, axis, pairs)]
    unnamed x11 -> x86, local copies, waits for them, and re-layouts: 23.5 us -> 18.9 us
  transfers between devices with their start and end apart: 6 -> 50, of which waited for: 4 -> 26; matrix products, arithmetic and copies ran while one was open for 17% -> 1% of each run, Pallas kernels for 0% -> 42%
where the time goes in v1:
time: 537 us; the launch traced here: 533 us
  Pallas kernels  225 us (42%)
  waiting for transfers between devices  212 us (39%)
  starting transfers between devices  40.7 us (8%)
  local copies, waits for them, and re-layouts  24.5 us (5%)
  between operations  16.6 us (3%)
  other arithmetic  12.8 us (2%)
    ppermute x44, waiting for transfers between devices, along(): return lambda value: lax.ppermute(value, axis, pairs)  205 us
    pallas_call x5, Pallas kernels, weight_chunk(): pl.pallas_call(body, grid_spec=pltpu.PrefetchScalarGridSpec(num_scalar_pr...  78.5 us
    pallas_call x2, Pallas kernels, input_part(): pl.pallas_call(body, grid_spec=pltpu.PrefetchScalarGridSpec(num_scalar_pr...  59.4 us
    pallas_call x16, Pallas kernels, sums(): pl.pallas_call(body, grid=(rows // tile,), in_specs=[spec(first) for firs...  44.2 us
    ppermute x44, starting transfers between devices, along(): return lambda value: lax.ppermute(value, axis, pairs)  40.3 us
    pallas_call x5, Pallas kernels, assemble(): pl.pallas_call(body, grid_spec=pltpu.PrefetchScalarGridSpec(num_scalar_pr...  20.3 us
    unnamed x86, local copies, waits for them, and re-layouts  18.9 us
    pallas_call x5, Pallas kernels, cut_columns(): pl.pallas_call(body, grid=(1,), in_specs=[pl.BlockSpec(source.shape, lamb...  13.3 us
  transfers between devices with their start and end apart: 50, of which 26 were waited for; matrix products, arithmetic and copies ran while one was open for 1% of the time, Pallas kernels for 42%

profile of v1, /device:TPU:0, one launch (start us, length us, event | category | flops | bytes accessed | tf_op | source)
XLA Modules:
  0.0 533.0 jit_solution(17047396430840883280)
XLA Ops:
  7.2 2.6 cut_columns.5
  11.0 10.3 %multiply_convert_fusion.own_ref.refs_1_ = bf16[896,3072]{1,0:T(8,128)(2,1)} fusion(bf16[896,3072]{1,0:T(8,128)(2,1)} %param.9, bf16[896,3072]{1,0:T(8,128)(2,1)} %param.8, f32[]{:T(128)} %bitcast.5), kind=kLoop, calls=%fused_computation.11 | loop fusion | flops 35782656 | bytes 16515076 | tf_op jit(solution)/shard_map/convert_element_type | solution.py:498
  24.4 1.7 dynamic-slice_bitcast_fusion
  27.3 2.6 cut_columns.6
  31.9 25.3 %input_part.2 = (bf16[1792,3072]{1,0:T(8,128)(2,1)}, bf16[1792,96]{1,0:T(8,128)(2,1)}, bf16[448,32]{1,0:T(8,128)(2,1)}, bf16[448,32]{1,0:T(8,128)(2,1)}, bf16[44...) custom-call(s32[5]{0:T(128)} %stack.60.slots_ref, bf16[896,3072]{1,0:T(8,128)(2,1)} %multiply_convert_fusion.own_ref.refs_1_, ...), custom_call_target="tpu_custom_call" | custom-call | flops 33822867456 | bytes 62914560 | tf_op jit(solution)/shard_map/input_part/pallas_call | solution.py:361
  57.3 1.8 pad_maximum_fusion.refs_0_
  59.1 6.6 %all-gather.8.cloned.1.call-done.refs_0_ = bf16[1792,512]{1,0:T(8,128)(2,1)} async-done(((bf16[448,512]{1,0:T(8,128)(2,1)}), bf16[1792,512]{1,0:T(8,128)(2,1)}) %all-gather.8.cloned.1.call-update) | async-done | bytes 1835024 | tf_op jit(solution)/shard_map/all_gather | solution.py:492
  65.8 13.3 %weight_chunk.5 = (bf16[512,768]{1,0:T(8,128)(2,1)}, bf16[512,768]{1,0:T(8,128)(2,1)}, bf16[512,384]{1,0:T(8,128)(2,1)}, bf16[512,384]{1,0:T(8,128)(2,1)}, bf16[...) custom-call(s32[10]{0:T(128)} %concatenate.6.choice_ref, bf16[1792,512]{1,0:T(8,128)(2,1)} %all-gather.8.cloned.1.call-done.refs_0_, ...), custom_call_target="tpu_custom_call" | custom-call | flops 16911433728 | bytes 47972352 | tf_op jit(solution)/shard_map/weight_chunk/pallas_call | solution.py:153
  79.1 2.9 cut_columns.7
  82.0 2.7 cut_columns.8
  85.0 1.5 collective-permute-start.1
  86.5 1.5 collective-permute-start.2
  88.0 2.6 cut_columns.9
  90.6 13.7 %collective-permute-done.1.refs_1_ = bf16[512,768]{1,0:T(8,128)(2,1)S(1)} collective-permute-done((bf16[512,768]{1,0:T(8,128)(2,1)S(1)}, bf16[512,768]{1,0:T(8,128)(2,1)S(1)}, u32[]{:S(2)}, u32[]{:S(2)}) %collective-permute-start.1) | collective-permute-done | bytes 786464 | tf_op jit(solution)/shard_map/ppermute | solution.py:473
  106.4 2.3 sums.16
  108.7 1.5 collective-permute-start.4
  110.8 7.8 %collective-permute-done.4.refs_2_ = bf16[512,384]{1,0:T(8,128)(2,1)S(1)} collective-permute-done((bf16[512,384]{1,0:T(8,128)(2,1)}, bf16[512,384]{1,0:T(8,128)(2,1)S(1)}, u32[]{:S(2)}, u32[]{:S(2)}) %collective-permute-start.4) | collective-permute-done | bytes 393248 | tf_op jit(solution)/shard_map/ppermute | solution.py:473
  120.6 2.6 sums.17.refs_3_.own_ref
  123.1 13.4 %weight_chunk.6 = (bf16[512,768]{1,0:T(8,128)(2,1)}, bf16[512,768]{1,0:T(8,128)(2,1)}, bf16[512,384]{1,0:T(8,128)(2,1)}, bf16[512,384]{1,0:T(8,128)(2,1)}, bf16[...) custom-call(s32[10]{0:T(128)} %concatenate.6.choice_ref, bf16[1792,512]{1,0:T(8,128)(2,1)} %all-gather.6.cloned.1.call-done.refs_0_, ...), custom_call_target="tpu_custom_call" | custom-call | flops 16911433728 | bytes 47972352 | tf_op jit(solution)/shard_map/weight_chunk/pallas_call | solution.py:153
  136.5 34.0 %input_part.3.refs_2_ = bf16[1792,3072]{1,0:T(8,128)(2,1)} custom-call(s32[5]{0:T(128)} %stack.60.slots_ref, bf16[896,3072]{1,0:T(8,128)(2,1)} %multiply_convert_fusion.own_ref.refs_1_, bf16[896,3072]{1,0:T(8,128)(2,1)} %collective-permute-done.other_ref.refs_2_, bf16[3072,3072]{1,0:T(8,128)(2,1)} %weight_ref.3, ...), custom_call_target="tpu_custom_call", output_to_operand_aliasing={{}: (7, {})} | custom-call | flops 67645734912 | bytes 92798976 | tf_op jit(solution)/shard_map/input_part/pallas_call | solution.py:361
  174.3 1.5 collective-permute-start.11
  175.8 16.4 %collective-permute-done.6.refs_1_.near_ref = bf16[512,768]{1,0:T(8,128)(2,1)S(1)} collective-permute-done((bf16[512,768]{1,0:T(8,128)(2,1)S(1)}, bf16[512,768]{1,0:T(8,128)(2,1)S(1)}, u32[]{:S(2)}, u32[]{:S(2)}) %collective-permute-start.6) | collective-permute-done | bytes 786464 | tf_op jit(solution)/shard_map/ppermute | solution.py:473
  194.0 2.0 sums.18
  197.7 11.3 %collective-permute-done.10.refs_1_ = bf16[512,768]{1,0:T(8,128)(2,1)S(1)} collective-permute-done((bf16[512,768]{1,0:T(8,128)(2,1)}, bf16[512,768]{1,0:T(8,128)(2,1)S(1)}, u32[]{:S(2)}, u32[]{:S(2)}) %collective-permute-start.10) | collective-permute-done | bytes 786464 | tf_op jit(solution)/shard_map/ppermute | solution.py:473
  210.0 2.3 sums.19
  214.0 3.4 collective-permute-done.8.refs_8_.low_ref
  218.3 5.1 collective-permute-done.12.refs_2_
  224.3 2.6 sums.20.refs_3_.own_ref
  227.0 19.5 %weight_chunk.7 = (bf16[768,768]{1,0:T(8,128)(2,1)}, bf16[768,768]{1,0:T(8,128)(2,1)}, bf16[768,384]{1,0:T(8,128)(2,1)}, bf16[768,384]{1,0:T(8,128)(2,1)}, bf16[...) custom-call(s32[10]{0:T(128)} %concatenate.6.choice_ref, ...), custom_call_target="tpu_custom_call" | custom-call | flops 29595009024 | bytes 59179008 | tf_op jit(solution)/shard_map/weight_chunk/pallas_call | solution.py:153
  249.2 1.4 collective-permute-start.16
  251.2 3.2 assemble.5.refs_4_.refs_0_
  254.4 4.1 low_term.1.refs_2_.refs_0_
  258.6 29.8 %collective-permute-done.15.refs_1_.near_ref = bf16[512,768]{1,0:T(8,128)(2,1)S(1)} collective-permute-done((bf16[512,768]{1,0:T(8,128)(2,1)}, bf16[512,768]{1,0:T(8,128)(2,1)S(1)}, u32[]{:S(2)}, u32[]{:S(2)}) %collective-permute-start.15) | collective-permute-done | bytes 786464 | tf_op jit(solution)/shard_map/ppermute | solution.py:473
  289.3 2.0 sums.21
  292.7 3.5 sums.22
  300.2 16.5 %collective-permute-done.17.refs_8_.low_ref = bf16[512,384]{1,0:T(8,128)(2,1)S(1)} collective-permute-done((bf16[512,384]{1,0:T(8,128)(2,1)}, bf16[512,384]{1,0:T(8,128)(2,1)S(1)}, u32[]{:S(2)}, u32[]{:S(2)}) %collective-permute-start.17) | collective-permute-done | bytes 393248 | tf_op jit(solution)/shard_map/ppermute | solution.py:473
  318.0 4.0 sums.23.refs_3_.own_ref
  323.7 17.3 %weight_chunk.8 = (bf16[768,768]{1,0:T(8,128)(2,1)}, bf16[768,768]{1,0:T(8,128)(2,1)}, bf16[768,384]{1,0:T(8,128)(2,1)}, bf16[768,384]{1,0:T(8,128)(2,1)}, bf16[...) custom-call(s32[10]{0:T(128)} %concatenate.6.choice_ref, bf16[1792,768]{1,0:T(8,128)(2,1)} %all-gather.14.cloned.1.call-done.refs_0_, ...), custom_call_target="tpu_custom_call" | custom-call | flops 25367150592 | bytes 55443456 | tf_op jit(solution)/shard_map/weight_chunk/pallas_call | solution.py:153
  341.0 1.7 collective-permute-start.24
  343.5 3.2 assemble.6.refs_2_.refs_0_
  346.7 12.9 %collective-permute-done.14.refs_1_ = bf16[32,3072]{1,0:T(8,128)(2,1)S(1)} collective-permute-done((bf16[32,3072]{1,0:T(8,128)(2,1)}, bf16[32,3072]{1,0:T(8,128)(2,1)S(1)}, u32[]{:S(2)}, u32[]{:S(2)}) %collective-permute-start.14) | collective-permute-done | bytes 196640 | tf_op jit(solution)/shard_map/ppermute | solution.py:473
  360.3 1.8 sums.24.refs_2_.first_ref
  364.2 3.2 sums.25
  367.3 3.9 collective-permute-done.24.refs_1_
  372.2 3.5 sums.26
  377.0 1.7 collective-permute-start.30
  380.9 20.5 %collective-permute-done.23.second_ref = bf16[32,3072]{1,0:T(8,128)(2,1)S(1)} collective-permute-done((bf16[32,3072]{1,0:T(8,128)(2,1)}, bf16[32,3072]{1,0:T(8,128)(2,1)S(1)}, u32[]{:S(2)}, u32[]{:S(2)}) %collective-permute-start.23) | collective-permute-done | bytes 196640 | tf_op jit(solution)/shard_map/ppermute | solution.py:473
  402.0 1.8 blocks_of.1.refs_6_.refs_3_
  405.3 3.9 sums.27.refs_5_.own_ref
  410.8 14.9 %weight_chunk.9 = (bf16[704,768]{1,0:T(8,128)(2,1)}, bf16[704,768]{1,0:T(8,128)(2,1)}, bf16[704,384]{1,0:T(8,128)(2,1)}, bf16[704,384]{1,0:T(8,128)(2,1)}, bf16[...) custom-call(s32[10]{0:T(128)} %concatenate.6.choice_ref, bf16[1792,512]{1,0:T(8,128)(2,1)} %all-gather.10.cloned.1.call-done.refs_0_, ...), custom_call_target="tpu_custom_call" | custom-call | flops 16911433728 | bytes 47972352 | tf_op jit(solution)/shard_map/weight_chunk/pallas_call | solution.py:153
  425.7 1.6 collective-permute-start.32
  428.3 5.4 %assemble.7.refs_2_.refs_0_ = bf16[3072,3072]{1,0:T(8,128)(2,1)} custom-call(s32[1]{0:T(128)} %bitcast.18.group_ref, bf16[768,768]{1,0:T(8,128)(2,1)} %sums.23.refs_3_.own_ref, bf16[768,768]{1,0:T(8,128)(2,1)} %copy-done.4, bf16[768,768]{1,0:T(8,128)(2,1)} %copy-done.3, bf16[768,384]{1,0:T(8,128)(2,1)} %copy-done.17, ...), custom_call_target="tpu_custom_call", output_to_operand_aliasing={{}: (6, {})} | custom-call | bytes 28311552 | tf_op jit(solution)/shard_map/assemble/pallas_call | solution.py:244
  433.7 4.7 collective-permute-done.34.refs_0_.far_ref
  440.5 3.2 sums.28
  445.1 17.6 %collective-permute-done.32.refs_1_ = bf16[704,768]{1,0:T(8,128)(2,1)} collective-permute-done((bf16[704,768]{1,0:T(8,128)(2,1)}, bf16[704,768]{1,0:T(8,128)(2,1)}, u32[]{:S(2)}, u32[]{:S(2)}) %collective-permute-start.32) | collective-permute-done | bytes 1081376 | tf_op jit(solution)/shard_map/ppermute | solution.py:473
  462.7 2.4 sums.29
  466.5 12.4 %collective-permute-done.36.refs_2_ = bf16[704,384]{1,0:T(8,128)(2,1)S(1)} collective-permute-done((bf16[704,384]{1,0:T(8,128)(2,1)}, bf16[704,384]{1,0:T(8,128)(2,1)S(1)}, u32[]{:S(2)}, u32[]{:S(2)}) %collective-permute-start.36) | collective-permute-done | bytes 540704 | tf_op jit(solution)/shard_map/ppermute | solution.py:473
  481.0 2.9 sums.30.refs_1_.own_ref
  485.2 5.4 %assemble.8.refs_2_.refs_0_ = bf16[3072,3072]{1,0:T(8,128)(2,1)} custom-call(s32[1]{0:T(128)} %bitcast.18.group_ref, bf16[768,768]{1,0:T(8,128)(2,1)} %sums.27.refs_5_.own_ref, bf16[768,768]{1,0:T(8,128)(2,1)} %copy-done.9, bf16[768,768]{1,0:T(8,128)(2,1)} %copy-done.8, bf16[768,384]{1,0:T(8,128)(2,1)} %copy-done.19, ...), custom_call_target="tpu_custom_call", output_to_operand_aliasing={{}: (6, {})} | custom-call | bytes 28311552 | tf_op jit(solution)/shard_map/assemble/pallas_call | solution.py:244
  490.5 13.3 %collective-permute-done.40.refs_1_.near_ref = bf16[704,768]{1,0:T(8,128)(2,1)S(1)} collective-permute-done((bf16[704,768]{1,0:T(8,128)(2,1)}, bf16[704,768]{1,0:T(8,128)(2,1)S(1)}, u32[]{:S(2)}, u32[]{:S(2)}) %collective-permute-start.40) | collective-permute-done | bytes 1081376 | tf_op jit(solution)/shard_map/ppermute | solution.py:473
  505.8 2.1 sums.31
  509.3 8.2 %collective-permute-done.42.low_ref = bf16[704,384]{1,0:T(8,128)(2,1)S(1)} collective-permute-done((bf16[704,384]{1,0:T(8,128)(2,1)}, bf16[704,384]{1,0:T(8,128)(2,1)S(1)}, u32[]{:S(2)}, u32[]{:S(2)}) %collective-permute-start.42) | collective-permute-done | bytes 540704 | tf_op jit(solution)/shard_map/ppermute | solution.py:473
  519.1 3.1 assemble.9.refs_0_
  522.2 3.8 adapter_totals.1
  (175 shorter events, 60.9 us)
Async XLA Ops:
  7.2 58.6 %all-gather.8.cloned.1.call-start = ((), (), s32[]{:S(2)}) async-start(), calls=%async_computation.2 | async-start | bytes 2293760 | tf_op jit(solution)/shard_map/all_gather | solution.py:492
  11.0 10.9 %copy-start.42 = (s32[4]{0:T(128)S(1)}, s32[4]{0:T(128)}, u32[]{:S(2)}) copy-start(s32[4]{0:T(128)} %param.13) | copy-start | bytes 52
  11.0 15.1 %copy-start = (bf16[448,3072]{1,0:T(8,128)(2,1)S(1)}, bf16[448,3072]{1,0:T(8,128)(2,1)}, u32[]{:S(2)}) copy-start(bf16[448,3072]{1,0:T(8,128)(2,1)} %refs_3_.1) | copy-start | bytes 8257540
  21.3 10.6 %collective-permute-start = (bf16[896,3072]{1,0:T(8,128)(2,1)}, bf16[896,3072]{1,0:T(8,128)(2,1)}, u32[]{:S(2)}, u32[]{:S(2)}) collective-permute-start(bf16[896,3072]{1,0:T(8,128)(2,1)} %multiply_convert_fusion.own_ref.refs_1_), channel_id=1, source_target_pairs={{0,1},{1,0},{2,3},{3,2},{4,5},{5,4},{6,7},{7,6},{8,9},{9,8},{10,11... | collective-permute-start | bytes 16515080 | tf_op jit(solution)/shard_map/ppermute | solution.py:473
  21.8 101.4 %all-gather.6.cloned.1.call-start = ((), (), s32[]{:S(2)}) async-start(), calls=%async_computation.1 | async-start | bytes 2293760 | tf_op jit(solution)/shard_map/all_gather | solution.py:492
  26.1 5.8 %copy-start.28 = (bf16[32,3072]{1,0:T(8,128)(2,1)}, bf16[32,3072]{1,0:T(8,128)(2,1)S(1)}, u32[]{:S(2)}) copy-start(bf16[32,3072]{1,0:T(8,128)(2,1)S(1)} %get-tuple-element.135.down_ref) | copy-start | bytes 589828
  27.1 4.7 collective-permute-start.3
  29.9 197.1 %all-gather.12.cloned.1.call-start = ((), (), s32[]{:S(2)}) async-start(), calls=%async_computation.5 | async-start | bytes 4014080 | tf_op jit(solution)/shard_map/all_gather | solution.py:492
  79.1 5.9 %copy-start.27 = (bf16[512,768]{1,0:T(8,128)(2,1)S(1)}, bf16[512,768]{1,0:T(8,128)(2,1)}, u32[]{:S(2)}) copy-start(bf16[512,768]{1,0:T(8,128)(2,1)} %get-tuple-element.75.refs_1_) | copy-start | bytes 2359300
  79.1 7.4 %copy-start.41 = (bf16[512,768]{1,0:T(8,128)(2,1)S(1)}, bf16[512,768]{1,0:T(8,128)(2,1)}, u32[]{:S(2)}) copy-start(bf16[512,768]{1,0:T(8,128)(2,1)} %get-tuple-element.78) | copy-start | bytes 2359300
  82.0 241.7 %all-gather.14.cloned.1.call-start = ((), (), s32[]{:S(2)}) async-start(), calls=%async_computation.6 | async-start | bytes 3440640 | tf_op jit(solution)/shard_map/all_gather | solution.py:492
  84.8 326.0 %all-gather.10.cloned.1.call-start = ((), (), s32[]{:S(2)}) async-start(), calls=%async_computation.4 | async-start | bytes 2293760 | tf_op jit(solution)/shard_map/all_gather | solution.py:492
  85.0 19.3 %collective-permute-start.1 = (bf16[512,768]{1,0:T(8,128)(2,1)S(1)}, bf16[512,768]{1,0:T(8,128)(2,1)S(1)}, u32[]{:S(2)}, u32[]{:S(2)}) collective-permute-start(bf16[512,768]{1,0:T(8,128)(2,1)S(1)} %copy-done.27), channel_id=1, source_target_pairs={{0,8},{8,0},{16,24},{24,16},{1,9},{9,1},{17,25},{25,17},{2,10},{10... | collective-permute-start | bytes 2359304 | tf_op jit(solution)/shard_map/ppermute | solution.py:473
  86.5 19.0 %collective-permute-start.2 = (bf16[512,768]{1,0:T(8,128)(2,1)S(1)}, bf16[512,768]{1,0:T(8,128)(2,1)S(1)}, u32[]{:S(2)}, u32[]{:S(2)}) collective-permute-start(bf16[512,768]{1,0:T(8,128)(2,1)S(1)} %copy-done.41), channel_id=1, source_target_pairs={{0,16},{8,24},{16,0},{24,8},{1,17},{9,25},{17,1},{25,9},{2,18},{10... | collective-permute-start | bytes 2359304 | tf_op jit(solution)/shard_map/ppermute | solution.py:473
  104.3 1.2 copy-start.13
  108.7 9.9 %collective-permute-start.4 = (bf16[512,384]{1,0:T(8,128)(2,1)}, bf16[512,384]{1,0:T(8,128)(2,1)S(1)}, u32[]{:S(2)}, u32[]{:S(2)}) collective-permute-start(bf16[512,384]{1,0:T(8,128)(2,1)} %get-tuple-element.85.refs_6_), channel_id=1, source_target_pairs={{0,16},{8,24},{16,0},{24,8},{1,17},{9,25},{17,1},{25,9},{2,18},{10... | collective-permute-start | bytes 1179656 | tf_op jit(solution)/shard_map/ppermute | solution.py:473
  110.1 9.7 %collective-permute-start.5 = (bf16[512,384]{1,0:T(8,128)(2,1)}, bf16[512,384]{1,0:T(8,128)(2,1)S(1)}, u32[]{:S(2)}, u32[]{:S(2)}) collective-permute-start(bf16[512,384]{1,0:T(8,128)(2,1)} %get-tuple-element.87.refs_7_), channel_id=1, source_target_pairs={{0,8},{8,0},{16,24},{24,16},{1,9},{9,1},{17,25},{25,17},{2,10},{10... | collective-permute-start | bytes 1179656 | tf_op jit(solution)/shard_map/ppermute | solution.py:473
  110.7 415.3 %reduce-scatter.2.cloned.1.call-start = ((), (), s32[]{:S(2)}) async-start(), calls=%async_computation.3 | async-start | bytes 13762560 | tf_op jit(solution)/shard_map/reduce_scatter | solution.py:582
  118.6 1.2 copy-start.35
  171.7 20.5 %collective-permute-start.6 = (bf16[512,768]{1,0:T(8,128)(2,1)S(1)}, bf16[512,768]{1,0:T(8,128)(2,1)S(1)}, u32[]{:S(2)}, u32[]{:S(2)}) collective-permute-start(bf16[512,768]{1,0:T(8,128)(2,1)S(1)} %copy-done.10), channel_id=1, source_target_pairs={{0,8},{8,0},{16,24},{24,16},{1,9},{9,1},{17,25},{25,17},{2,10},{10... | collective-permute-start | bytes 2359304 | tf_op jit(solution)/shard_map/ppermute | solution.py:473
  172.6 20.5 %collective-permute-start.7 = (bf16[512,768]{1,0:T(8,128)(2,1)S(1)}, bf16[512,768]{1,0:T(8,128)(2,1)S(1)}, u32[]{:S(2)}, u32[]{:S(2)}) collective-permute-start(bf16[512,768]{1,0:T(8,128)(2,1)S(1)} %copy-done.10), channel_id=1, source_target_pairs={{0,16},{8,24},{16,0},{24,8},{1,17},{9,25},{17,1},{25,9},{2,18},{10... | collective-permute-start | bytes 2359304 | tf_op jit(solution)/shard_map/ppermute | solution.py:473
  173.1 35.9 %collective-permute-start.10 = (bf16[512,768]{1,0:T(8,128)(2,1)}, bf16[512,768]{1,0:T(8,128)(2,1)S(1)}, u32[]{:S(2)}, u32[]{:S(2)}) collective-permute-start(bf16[512,768]{1,0:T(8,128)(2,1)} %get-tuple-element.88.refs_2_), channel_id=1, source_target_pairs={{0,8},{8,0},{16,24},{24,16},{1,9},{9,1},{17,25},{25,17},{2,10},{10... | collective-permute-start | bytes 2359304 | tf_op jit(solution)/shard_map/ppermute | solution.py:473
  174.3 35.7 %collective-permute-start.11 = (bf16[512,768]{1,0:T(8,128)(2,1)}, bf16[512,768]{1,0:T(8,128)(2,1)}, u32[]{:S(2)}, u32[]{:S(2)}) collective-permute-start(bf16[512,768]{1,0:T(8,128)(2,1)} %get-tuple-element.89.refs_3_), channel_id=1, source_target_pairs={{0,16},{8,24},{16,0},{24,8},{1,17},{9,25},{17,1},{25,9},{2,18},{10... | collective-permute-start | bytes 2359304 | tf_op jit(solution)/shard_map/ppermute | solution.py:473
  196.0 21.4 %collective-permute-start.8 = (bf16[512,384]{1,0:T(8,128)(2,1)}, bf16[512,384]{1,0:T(8,128)(2,1)S(1)}, u32[]{:S(2)}, u32[]{:S(2)}) collective-permute-start(bf16[512,384]{1,0:T(8,128)(2,1)} %get-tuple-element.91.refs_4_), channel_id=1, source_target_pairs={{0,8},{8,0},{16,24},{24,16},{1,9},{9,1},{17,25},{25,17},{2,10},{10... | collective-permute-start | bytes 1179656 | tf_op jit(solution)/shard_map/ppermute | solution.py:473
  197.1 21.2 %collective-permute-start.9 = (bf16[512,384]{1,0:T(8,128)(2,1)}, bf16[512,384]{1,0:T(8,128)(2,1)S(1)}, u32[]{:S(2)}, u32[]{:S(2)}) collective-permute-start(bf16[512,384]{1,0:T(8,128)(2,1)} %get-tuple-element.92.refs_5_), channel_id=1, source_target_pairs={{0,16},{8,24},{16,0},{24,8},{1,17},{9,25},{17,1},{25,9},{2,18},{10... | collective-permute-start | bytes 1179656 | tf_op jit(solution)/shard_map/ppermute | solution.py:473
  212.3 11.1 %collective-permute-start.12 = (bf16[512,384]{1,0:T(8,128)(2,1)}, bf16[512,384]{1,0:T(8,128)(2,1)S(1)}, u32[]{:S(2)}, u32[]{:S(2)}) collective-permute-start(bf16[512,384]{1,0:T(8,128)(2,1)} %get-tuple-element.96.refs_6_), channel_id=1, source_target_pairs={{0,16},{8,24},{16,0},{24,8},{1,17},{9,25},{17,1},{25,9},{2,18},{10... | collective-permute-start | bytes 1179656 | tf_op jit(solution)/shard_map/ppermute | solution.py:473
  212.8 10.6 %collective-permute-start.13 = (bf16[512,384]{1,0:T(8,128)(2,1)}, bf16[512,384]{1,0:T(8,128)(2,1)S(1)}, u32[]{:S(2)}, u32[]{:S(2)}) collective-permute-start(bf16[512,384]{1,0:T(8,128)(2,1)} %get-tuple-element.98.refs_7_), channel_id=1, source_target_pairs={{0,8},{8,0},{16,24},{24,16},{1,9},{9,1},{17,25},{25,17},{2,10},{10... | collective-permute-start | bytes 1179656 | tf_op jit(solution)/shard_map/ppermute | solution.py:473
  217.5 6.0 %copy-start.25 = (bf16[512,384]{1,0:T(8,128)(2,1)}, bf16[512,384]{1,0:T(8,128)(2,1)S(1)}, u32[]{:S(2)}) copy-start(bf16[512,384]{1,0:T(8,128)(2,1)S(1)} %collective-permute-done.8.refs_8_.low_ref) | copy-start | bytes 1179652
  218.3 5.1 copy-start.26
  246.5 44.8 %collective-permute-start.19 = (bf16[768,768]{1,0:T(8,128)(2,1)}, bf16[768,768]{1,0:T(8,128)(2,1)S(1)}, u32[]{:S(2)}, u32[]{:S(2)}) collective-permute-start(bf16[768,768]{1,0:T(8,128)(2,1)} %get-tuple-element.99.refs_0_), channel_id=1, source_target_pairs={{0,8},{8,0},{16,24},{24,16},{1,9},{9,1},{17,25},{25,17},{2,10},{10... | collective-permute-start | bytes 3538952 | tf_op jit(solution)/shard_map/ppermute | solution.py:473
  247.4 43.8 %collective-permute-start.20 = (bf16[768,768]{1,0:T(8,128)(2,1)}, bf16[768,768]{1,0:T(8,128)(2,1)S(1)}, u32[]{:S(2)}, u32[]{:S(2)}) collective-permute-start(bf16[768,768]{1,0:T(8,128)(2,1)} %get-tuple-element.105), channel_id=1, source_target_pairs={{0,16},{8,24},{16,0},{24,8},{1,17},{9,25},{17,1},{25,9},{2,18},{10... | collective-permute-start | bytes 3538952 | tf_op jit(solution)/shard_map/ppermute | solution.py:473
  248.0 40.3 %collective-permute-start.15 = (bf16[512,768]{1,0:T(8,128)(2,1)}, bf16[512,768]{1,0:T(8,128)(2,1)S(1)}, u32[]{:S(2)}, u32[]{:S(2)}) collective-permute-start(bf16[512,768]{1,0:T(8,128)(2,1)} %sums.20.refs_3_.own_ref), channel_id=1, source_target_pairs={{0,8},{8,0},{16,24},{24,16},{1,9},{9,1},{17,25},{25,17},{2,10},{10... | collective-permute-start | bytes 2359304 | tf_op jit(solution)/shard_map/ppermute | solution.py:473
  249.2 39.6 %collective-permute-start.16 = (bf16[512,768]{1,0:T(8,128)(2,1)}, bf16[512,768]{1,0:T(8,128)(2,1)}, u32[]{:S(2)}, u32[]{:S(2)}) collective-permute-start(bf16[512,768]{1,0:T(8,128)(2,1)} %sums.20.refs_3_.own_ref), channel_id=1, source_target_pairs={{0,16},{8,24},{16,0},{24,8},{1,17},{9,25},{17,1},{25,9},{2,18},{10... | collective-permute-start | bytes 2359304 | tf_op jit(solution)/shard_map/ppermute | solution.py:473
  291.3 1.4 copy-start.7
  296.2 20.6 %collective-permute-start.21 = (bf16[768,384]{1,0:T(8,128)(2,1)}, bf16[768,384]{1,0:T(8,128)(2,1)S(1)}, u32[]{:S(2)}, u32[]{:S(2)}) collective-permute-start(bf16[768,384]{1,0:T(8,128)(2,1)} %get-tuple-element.106.refs_6_), channel_id=1, source_target_pairs={{0,16},{8,24},{16,0},{24,8},{1,17},{9,25},{17,1},{25,9},{2,18},{10... | collective-permute-start | bytes 1769480 | tf_op jit(solution)/shard_map/ppermute | solution.py:473
  297.0 19.8 %collective-permute-start.22 = (bf16[768,384]{1,0:T(8,128)(2,1)}, bf16[768,384]{1,0:T(8,128)(2,1)S(1)}, u32[]{:S(2)}, u32[]{:S(2)}) collective-permute-start(bf16[768,384]{1,0:T(8,128)(2,1)} %get-tuple-element.108.refs_7_), channel_id=1, source_target_pairs={{0,8},{8,0},{16,24},{24,16},{1,9},{9,1},{17,25},{25,17},{2,10},{10... | collective-permute-start | bytes 1769480 | tf_op jit(solution)/shard_map/ppermute | solution.py:473
  297.9 18.8 %collective-permute-start.17 = (bf16[512,384]{1,0:T(8,128)(2,1)}, bf16[512,384]{1,0:T(8,128)(2,1)S(1)}, u32[]{:S(2)}, u32[]{:S(2)}) collective-permute-start(bf16[512,384]{1,0:T(8,128)(2,1)} %get-tuple-element.100.refs_4_), channel_id=1, source_target_pairs={{0,8},{8,0},{16,24},{24,16},{1,9},{9,1},{17,25},{25,17},{2,10},{10... | collective-permute-start | bytes 1179656 | tf_op jit(solution)/shard_map/ppermute | solution.py:473
  299.0 17.7 %collective-permute-start.18 = (bf16[512,384]{1,0:T(8,128)(2,1)}, bf16[512,384]{1,0:T(8,128)(2,1)S(1)}, u32[]{:S(2)}, u32[]{:S(2)}) collective-permute-start(bf16[512,384]{1,0:T(8,128)(2,1)} %get-tuple-element.101.refs_5_), channel_id=1, source_target_pairs={{0,16},{8,24},{16,0},{24,8},{1,17},{9,25},{17,1},{25,9},{2,18},{10... | collective-permute-start | bytes 1179656 | tf_op jit(solution)/shard_map/ppermute | solution.py:473
  316.8 1.2 copy-start.32
  322.0 40.0 %collective-permute-start.26 = (bf16[768,768]{1,0:T(8,128)(2,1)}, bf16[768,768]{1,0:T(8,128)(2,1)S(1)}, u32[]{:S(2)}, u32[]{:S(2)}) collective-permute-start(bf16[768,768]{1,0:T(8,128)(2,1)} %sums.23.refs_3_.own_ref), channel_id=1, source_target_pairs={{0,16},{8,24},{16,0},{24,8},{1,17},{9,25},{17,1},{25,9},{2,18},{10... | collective-permute-start | bytes 3538952 | tf_op jit(solution)/shard_map/ppermute | solution.py:473
  323.2 38.8 %collective-permute-start.27 = (bf16[768,768]{1,0:T(8,128)(2,1)}, bf16[768,768]{1,0:T(8,128)(2,1)S(1)}, u32[]{:S(2)}, u32[]{:S(2)}) collective-permute-start(bf16[768,768]{1,0:T(8,128)(2,1)} %sums.23.refs_3_.own_ref), channel_id=1, source_target_pairs={{0,8},{8,0},{16,24},{24,16},{1,9},{9,1},{17,25},{25,17},{2,10},{10... | collective-permute-start | bytes 3538952 | tf_op jit(solution)/shard_map/ppermute | solution.py:473
  341.0 30.2 %collective-permute-start.24 = (bf16[768,768]{1,0:T(8,128)(2,1)}, bf16[768,768]{1,0:T(8,128)(2,1)S(1)}, u32[]{:S(2)}, u32[]{:S(2)}) collective-permute-start(bf16[768,768]{1,0:T(8,128)(2,1)} %get-tuple-element.109.refs_1_), channel_id=1, source_target_pairs={{0,8},{8,0},{16,24},{24,16},{1,9},{9,1},{17,25},{25,17},{2,10},{10... | collective-permute-start | bytes 3538952 | tf_op jit(solution)/shard_map/ppermute | solution.py:473
  342.7 28.6 %collective-permute-start.25 = (bf16[768,768]{1,0:T(8,128)(2,1)}, bf16[768,768]{1,0:T(8,128)(2,1)}, u32[]{:S(2)}, u32[]{:S(2)}) collective-permute-start(bf16[768,768]{1,0:T(8,128)(2,1)} %get-tuple-element.112), channel_id=1, source_target_pairs={{0,16},{8,24},{16,0},{24,8},{1,17},{9,25},{17,1},{25,9},{2,18},{10... | collective-permute-start | bytes 3538952 | tf_op jit(solution)/shard_map/ppermute | solution.py:473
  343.5 16.1 %collective-permute-start.14 = (bf16[32,3072]{1,0:T(8,128)(2,1)}, bf16[32,3072]{1,0:T(8,128)(2,1)S(1)}, u32[]{:S(2)}, u32[]{:S(2)}) collective-permute-start(bf16[32,3072]{1,0:T(8,128)(2,1)} %low_term.1.refs_2_.refs_0_), channel_id=1, source_target_pairs={{0,2},{2,0},{4,6},{6,4},{1,3},{3,1},{5,7},{7,5},{8,10},{10,8},{12,... | collective-permute-start | bytes 589832 | tf_op jit(solution)/shard_map/ppermute | solution.py:473
  375.7 28.1 %collective-permute-start.28 = (bf16[768,384]{1,0:T(8,128)(2,1)}, bf16[768,384]{1,0:T(8,128)(2,1)S(1)}, u32[]{:S(2)}, u32[]{:S(2)}) collective-permute-start(bf16[768,384]{1,0:T(8,128)(2,1)} %get-tuple-element.115.refs_0_), channel_id=1, source_target_pairs={{0,16},{8,24},{16,0},{24,8},{1,17},{9,25},{17,1},{25,9},{2,18},{10... | collective-permute-start | bytes 1769480 | tf_op jit(solution)/shard_map/ppermute | solution.py:473
  376.7 27.2 %collective-permute-start.29 = (bf16[768,384]{1,0:T(8,128)(2,1)}, bf16[768,384]{1,0:T(8,128)(2,1)S(1)}, u32[]{:S(2)}, u32[]{:S(2)}) collective-permute-start(bf16[768,384]{1,0:T(8,128)(2,1)} %get-tuple-element.116.refs_1_), channel_id=1, source_target_pairs={{0,8},{8,0},{16,24},{24,16},{1,9},{9,1},{17,25},{25,17},{2,10},{10... | collective-permute-start | bytes 1769480 | tf_op jit(solution)/shard_map/ppermute | solution.py:473
  377.0 26.9 %collective-permute-start.30 = (bf16[768,384]{1,0:T(8,128)(2,1)}, bf16[768,384]{1,0:T(8,128)(2,1)S(1)}, u32[]{:S(2)}, u32[]{:S(2)}) collective-permute-start(bf16[768,384]{1,0:T(8,128)(2,1)} %get-tuple-element.113.refs_4_), channel_id=1, source_target_pairs={{0,8},{8,0},{16,24},{24,16},{1,9},{9,1},{17,25},{25,17},{2,10},{10... | collective-permute-start | bytes 1769480 | tf_op jit(solution)/shard_map/ppermute | solution.py:473
  378.7 25.2 %collective-permute-start.31 = (bf16[768,384]{1,0:T(8,128)(2,1)}, bf16[768,384]{1,0:T(8,128)(2,1)S(1)}, u32[]{:S(2)}, u32[]{:S(2)}) collective-permute-start(bf16[768,384]{1,0:T(8,128)(2,1)} %get-tuple-element.114.refs_5_), channel_id=1, source_target_pairs={{0,16},{8,24},{16,0},{24,8},{1,17},{9,25},{17,1},{25,9},{2,18},{10... | collective-permute-start | bytes 1769480 | tf_op jit(solution)/shard_map/ppermute | solution.py:473
  379.8 21.6 %collective-permute-start.23 = (bf16[32,3072]{1,0:T(8,128)(2,1)}, bf16[32,3072]{1,0:T(8,128)(2,1)S(1)}, u32[]{:S(2)}, u32[]{:S(2)}) collective-permute-start(bf16[32,3072]{1,0:T(8,128)(2,1)} %sums.24.refs_2_.first_ref), channel_id=1, source_target_pairs={{0,4},{2,6},{4,0},{6,2},{1,5},{3,7},{5,1},{7,3},{8,12},{10,14},{12... | collective-permute-start | bytes 589832 | tf_op jit(solution)/shard_map/ppermute | solution.py:473
  403.9 1.3 copy-start.17
  403.9 1.4 copy-start.18
  409.3 29.1 %collective-permute-start.34 = (bf16[768,768]{1,0:T(8,128)(2,1)}, bf16[768,768]{1,0:T(8,128)(2,1)S(1)}, u32[]{:S(2)}, u32[]{:S(2)}) collective-permute-start(bf16[768,768]{1,0:T(8,128)(2,1)} %sums.27.refs_5_.own_ref), channel_id=1, source_target_pairs={{0,16},{8,24},{16,0},{24,8},{1,17},{9,25},{17,1},{25,9},{2,18},{10... | collective-permute-start | bytes 3538952 | tf_op jit(solution)/shard_map/ppermute | solution.py:473
  410.3 29.1 %collective-permute-start.35 = (bf16[768,768]{1,0:T(8,128)(2,1)}, bf16[768,768]{1,0:T(8,128)(2,1)S(1)}, u32[]{:S(2)}, u32[]{:S(2)}) collective-permute-start(bf16[768,768]{1,0:T(8,128)(2,1)} %sums.27.refs_5_.own_ref), channel_id=1, source_target_pairs={{0,8},{8,0},{16,24},{24,16},{1,9},{9,1},{17,25},{25,17},{2,10},{10... | collective-permute-start | bytes 3538952 | tf_op jit(solution)/shard_map/ppermute | solution.py:473
  425.7 37.0 %collective-permute-start.32 = (bf16[704,768]{1,0:T(8,128)(2,1)}, bf16[704,768]{1,0:T(8,128)(2,1)}, u32[]{:S(2)}, u32[]{:S(2)}) collective-permute-start(bf16[704,768]{1,0:T(8,128)(2,1)} %get-tuple-element.121.refs_1_), channel_id=1, source_target_pairs={{0,8},{8,0},{16,24},{24,16},{1,9},{9,1},{17,25},{25,17},{2,10},{10... | collective-permute-start | bytes 3244040 | tf_op jit(solution)/shard_map/ppermute | solution.py:473
  427.3 35.4 %collective-permute-start.33 = (bf16[704,768]{1,0:T(8,128)(2,1)}, bf16[704,768]{1,0:T(8,128)(2,1)}, u32[]{:S(2)}, u32[]{:S(2)}) collective-permute-start(bf16[704,768]{1,0:T(8,128)(2,1)} %get-tuple-element.124), channel_id=1, source_target_pairs={{0,16},{8,24},{16,0},{24,8},{1,17},{9,25},{17,1},{25,9},{2,18},{10... | collective-permute-start | bytes 3244040 | tf_op jit(solution)/shard_map/ppermute | solution.py:473
  443.6 36.1 %collective-permute-start.38 = (bf16[768,384]{1,0:T(8,128)(2,1)}, bf16[768,384]{1,0:T(8,128)(2,1)S(1)}, u32[]{:S(2)}, u32[]{:S(2)}) collective-permute-start(bf16[768,384]{1,0:T(8,128)(2,1)} %get-tuple-element.125.refs_4_), channel_id=1, source_target_pairs={{0,8},{8,0},{16,24},{24,16},{1,9},{9,1},{17,25},{25,17},{2,10},{10... | collective-permute-start | bytes 1769480 | tf_op jit(solution)/shard_map/ppermute | solution.py:473
  444.1 35.7 %collective-permute-start.39 = (bf16[768,384]{1,0:T(8,128)(2,1)}, bf16[768,384]{1,0:T(8,128)(2,1)S(1)}, u32[]{:S(2)}, u32[]{:S(2)}) collective-permute-start(bf16[768,384]{1,0:T(8,128)(2,1)} %get-tuple-element.126.refs_5_), channel_id=1, source_target_pairs={{0,16},{8,24},{16,0},{24,8},{1,17},{9,25},{17,1},{25,9},{2,18},{10... | collective-permute-start | bytes 1769480 | tf_op jit(solution)/shard_map/ppermute | solution.py:473
  465.1 13.8 %collective-permute-start.36 = (bf16[704,384]{1,0:T(8,128)(2,1)}, bf16[704,384]{1,0:T(8,128)(2,1)S(1)}, u32[]{:S(2)}, u32[]{:S(2)}) collective-permute-start(bf16[704,384]{1,0:T(8,128)(2,1)} %get-tuple-element.127.refs_6_), channel_id=1, source_target_pairs={{0,16},{8,24},{16,0},{24,8},{1,17},{9,25},{17,1},{25,9},{2,18},{10... | collective-permute-start | bytes 1622024 | tf_op jit(solution)/shard_map/ppermute | solution.py:473
  466.1 13.6 %collective-permute-start.37 = (bf16[704,384]{1,0:T(8,128)(2,1)}, bf16[704,384]{1,0:T(8,128)(2,1)S(1)}, u32[]{:S(2)}, u32[]{:S(2)}) collective-permute-start(bf16[704,384]{1,0:T(8,128)(2,1)} %get-tuple-element.129.refs_7_), channel_id=1, source_target_pairs={{0,8},{8,0},{16,24},{24,16},{1,9},{9,1},{17,25},{25,17},{2,10},{10... | collective-permute-start | bytes 1622024 | tf_op jit(solution)/shard_map/ppermute | solution.py:473
  479.8 1.2 copy-start.20
  483.8 20.0 %collective-permute-start.40 = (bf16[704,768]{1,0:T(8,128)(2,1)}, bf16[704,768]{1,0:T(8,128)(2,1)S(1)}, u32[]{:S(2)}, u32[]{:S(2)}) collective-permute-start(bf16[704,768]{1,0:T(8,128)(2,1)} %sums.30.refs_1_.own_ref), channel_id=1, source_target_pairs={{0,8},{8,0},{16,24},{24,16},{1,9},{9,1},{17,25},{25,17},{2,10},{10... | collective-permute-start | bytes 3244040 | tf_op jit(solution)/shard_map/ppermute | solution.py:473
  484.2 19.6 %collective-permute-start.41 = (bf16[704,768]{1,0:T(8,128)(2,1)}, bf16[704,768]{1,0:T(8,128)(2,1)S(1)}, u32[]{:S(2)}, u32[]{:S(2)}) collective-permute-start(bf16[704,768]{1,0:T(8,128)(2,1)} %sums.30.refs_1_.own_ref), channel_id=1, source_target_pairs={{0,16},{8,24},{16,0},{24,8},{1,17},{9,25},{17,1},{25,9},{2,18},{10... | collective-permute-start | bytes 3244040 | tf_op jit(solution)/shard_map/ppermute | solution.py:473
  507.9 9.6 %collective-permute-start.42 = (bf16[704,384]{1,0:T(8,128)(2,1)}, bf16[704,384]{1,0:T(8,128)(2,1)S(1)}, u32[]{:S(2)}, u32[]{:S(2)}) collective-permute-start(bf16[704,384]{1,0:T(8,128)(2,1)} %get-tuple-element.130.refs_1_), channel_id=1, source_target_pairs={{0,8},{8,0},{16,24},{24,16},{1,9},{9,1},{17,25},{25,17},{2,10},{10... | collective-permute-start | bytes 1622024 | tf_op jit(solution)/shard_map/ppermute | solution.py:473
  508.4 9.6 %collective-permute-start.43 = (bf16[704,384]{1,0:T(8,128)(2,1)}, bf16[704,384]{1,0:T(8,128)(2,1)S(1)}, u32[]{:S(2)}, u32[]{:S(2)}) collective-permute-start(bf16[704,384]{1,0:T(8,128)(2,1)} %get-tuple-element.131.refs_2_), channel_id=1, source_target_pairs={{0,16},{8,24},{16,0},{24,8},{1,17},{9,25},{17,1},{25,9},{2,18},{10... | collective-permute-start | bytes 1622024 | tf_op jit(solution)/shard_map/ppermute | solution.py:473
  (29 other events, 26.7 us)
Sparse Core Ops, SparseCore 0:
  21.9 43.8 all-gather.7
  67.9 40.2 all-gather.5
  110.3 63.4 all-gather.11
  175.3 55.6 all-gather.13
  232.3 40.1 all-gather.9
  275.3 193.7 reduce-scatter.1
